TPU v7x, 32 devices: a whole 2x2x4 slice. The times are simulated.
32 devices in a mesh: row: 4 (over z), col: 4 (over y, x), dp: 2 (over core).
Axes of the slice: x: 2, y: 2, z: 4, core: 2. Of those that a mesh axis runs over, the one named last changes fastest.
Arguments:
- tokens: bfloat16 [1024, 4096], P(('col', 'dp'), 'row'), may hold values from -6 to 6
- timesteps: int32 [4], replicated, may hold values from 0 to 999
- ada_weight: bfloat16 [3, 4096, 4096], P(None, 'col', 'row'), may hold values from -0.09375 to 0.09375
- up_weight: bfloat16 [4096, 16384], P('row', 'col'), may hold values from -0.90625 to 0.90625
- down_weight: bfloat16 [16384, 4096], P('col', 'row'), may hold values from -0.046875 to 0.046875
- cotangent: bfloat16 [1024, 4096], P(('col', 'dp'), 'row'), may hold values from -6 to 6
Outputs:
- grad_tokens: bfloat16 [1024, 4096], P(('col', 'dp'), 'row')
- grad_ada: float32 [3, 4096, 4096], P(None, 'col', 'row')
- grad_up: float32 [4096, 16384], P('row', ('col', 'dp'))
- grad_down: float32 [16384, 4096], P(('col', 'dp'), 'row')
All inputs are finite; a program needn't handle non-finite values.
Results may differ from a plain program's by a relative error of at most 0.04.
Values may be sent and summed in bfloat16 or wider, within the bound.
A program may use at most 192 MiB of HBM per device.

v0:
```python
import math

import jax
import jax.numpy as jnp
from jax import lax
from jax.sharding import PartitionSpec as P

tanh_scale = math.sqrt(2.0 / math.pi)


def gelu_tanh(h):
    return 0.5 * h * (1.0 + jnp.tanh(tanh_scale * (h + 0.044715 * h * h * h)))


def gelu_slope(h):
    inner = jnp.tanh(tanh_scale * (h + 0.044715 * h * h * h))
    return 0.5 * (1.0 + inner) + 0.5 * h * (1.0 - inner * inner) * tanh_scale * (
        1.0 + 3.0 * 0.044715 * h * h
    )


def time_features(timesteps, width):
    half = width // 2
    freqs = jnp.exp(-math.log(10000.0) * jnp.arange(half, dtype=jnp.float32) / half)
    angles = timesteps.astype(jnp.float32)[:, None] * freqs[None, :]
    embed = jnp.concatenate([jnp.cos(angles), jnp.sin(angles)], axis=1)
    return jax.nn.silu(embed).astype(jnp.bfloat16)


def body(tokens, timesteps, ada_weight, up_weight, down_weight, cotangent):
    rows_count = lax.axis_size("row")
    cols_count = lax.axis_size("col")
    col_index = lax.axis_index("col")
    tok_rows, width = tokens.shape
    full_width = width * rows_count
    in_width = ada_weight.shape[1]
    cond = time_features(timesteps, full_width)
    cond_part = lax.dynamic_slice_in_dim(cond, col_index * in_width, in_width, 1)
    mod_terms = jnp.einsum("vi,kio->vko", cond_part, ada_weight, preferred_element_type=jnp.float32)
    mod = lax.psum(mod_terms.astype(jnp.bfloat16), "col").astype(jnp.float32)
    own_mod = lax.dynamic_index_in_dim(mod, col_index, 0, keepdims=False)
    shift = own_mod[0]
    scale = own_mod[1]
    gate = own_mod[2]
    x = tokens.astype(jnp.float32)
    total, squares = lax.psum((jnp.sum(x, axis=1), jnp.sum(x * x, axis=1)), "row")
    mean = total / full_width
    var = squares / full_width - mean * mean
    rstd = lax.rsqrt(var + 1e-06)
    normed = (x - mean[:, None]) * rstd[:, None]
    modulated = (normed * (1.0 + scale) + shift).astype(jnp.bfloat16)
    mod_full = lax.all_gather(modulated, "col", axis=0, tiled=True)
    picked = mod_full
    hidden_own = lax.psum_scatter(
        jnp.dot(picked, up_weight, preferred_element_type=jnp.float32).astype(jnp.bfloat16),
        "row",
        scatter_dimension=0,
        tiled=True,
    ).astype(jnp.float32)
    act_own = gelu_tanh(hidden_own).astype(jnp.bfloat16)
    act_full = lax.all_gather(act_own, "row", axis=0, tiled=True)
    picked = act_full
    branch = lax.psum_scatter(
        jnp.dot(picked, down_weight, preferred_element_type=jnp.float32).astype(jnp.bfloat16),
        "col",
        scatter_dimension=0,
        tiled=True,
    ).astype(jnp.float32)
    cot = cotangent.astype(jnp.float32)
    grad_branch = (cot * gate).astype(jnp.bfloat16)
    grad_gate = jnp.sum(cot * branch, axis=0)
    branch_full = lax.all_gather(grad_branch, "col", axis=0, tiled=True)
    mod_full = lax.all_gather(modulated, "col", axis=0, tiled=True)
    act_full = lax.all_gather(act_own, "row", axis=0, tiled=True)
    down_part = lax.dot_general(
        act_full, branch_full, (((0,), (0,)), ((), ())), preferred_element_type=jnp.float32
    )
    picked = branch_full
    grad_act = lax.psum_scatter(
        lax.dot_general(
            picked, down_weight, (((1,), (1,)), ((), ())), preferred_element_type=jnp.float32
        ).astype(jnp.bfloat16),
        "row",
        scatter_dimension=0,
        tiled=True,
    ).astype(jnp.float32)
    grad_hidden = (grad_act * gelu_slope(hidden_own)).astype(jnp.bfloat16)
    grad_full = lax.all_gather(grad_hidden, "row", axis=0, tiled=True)
    up_part = lax.dot_general(
        mod_full, grad_full, (((0,), (0,)), ((), ())), preferred_element_type=jnp.float32
    )
    picked = grad_full
    grad_mod_in = lax.psum_scatter(
        lax.dot_general(
            picked, up_weight, (((1,), (1,)), ((), ())), preferred_element_type=jnp.float32
        ).astype(jnp.bfloat16),
        "col",
        scatter_dimension=0,
        tiled=True,
    ).astype(jnp.float32)
    grad_up, grad_down = (
        lax.psum_scatter(
            up_part.astype(jnp.bfloat16), "dp", scatter_dimension=1, tiled=True
        ).astype(jnp.float32),
        lax.psum_scatter(
            down_part.astype(jnp.bfloat16), "dp", scatter_dimension=0, tiled=True
        ).astype(jnp.float32),
    )
    grad_norm = grad_mod_in * (1.0 + scale)
    first, second = lax.psum(
        (jnp.sum(grad_norm, axis=1), jnp.sum(grad_norm * normed, axis=1)), "row"
    )
    first = first / full_width
    second = second / full_width
    grad_tokens = cot + rstd[:, None] * (grad_norm - first[:, None] - normed * second[:, None])
    own_grad = jnp.stack(
        [jnp.sum(grad_mod_in, axis=0), jnp.sum(grad_mod_in * normed, axis=0), grad_gate], axis=0
    )
    selector = (jnp.arange(cols_count, dtype=jnp.int32) == col_index).astype(jnp.float32)
    placed = selector[:, None, None] * own_grad[None, :, :]
    grad_mod = lax.psum(placed.astype(jnp.bfloat16), ("col", "dp")).astype(jnp.float32)
    grad_ada = jnp.einsum(
        "vi,vko->kio", cond_part.astype(jnp.float32), grad_mod, precision=lax.Precision.HIGHEST
    )
    return (grad_tokens.astype(jnp.bfloat16), grad_ada, grad_up, grad_down)


def solution(mesh):
    return jax.shard_map(
        body,
        mesh=mesh,
        in_specs=(
            P(("col", "dp"), "row"),
            P(),
            P(None, "col", "row"),
            P("row", "col"),
            P("col", "row"),
            P(("col", "dp"), "row"),
        ),
        out_specs=(
            P(("col", "dp"), "row"),
            P(None, "col", "row"),
            P("row", ("col", "dp")),
            P(("col", "dp"), "row"),
        ),
        check_vma=False,
    )
```

profile of v0, /device:TPU:0, one launch (start us, length us, event | category | flops | bytes accessed | tf_op | source)
XLA Modules:
  0.0 550.0 jit_solution(17634550768493690698)
XLA Ops:
  7.2 0.0 copy-start
  7.2 0.0 copy-start.1
  7.2 0.0 all-gather.7.cloned.1.call-start
  7.3 0.7 convert_element_type.83
  8.0 0.3 multiply_cosine_fusion
  8.3 3.7 convolution_convert_fusion.6
  12.0 17.7 %psum.44 = bf16[4,3,1024]{2,0,1:T(4,128)(2,1)S(1)} all-reduce(bf16[4,3,1024]{2,0,1:T(4,128)(2,1)S(1)} %convolution_convert_fusion.6), channel_id=1, replica_groups=mesh['row'=4,'col'=4,'dp'=2] {'col'}, use_global_device_ids=true, to_apply=%region_4.5 | all-reduce | flops 12288 | bytes 49152 | tf_op jit(solution)/shard_map/psum | solution.py:40
  29.7 0.0 copy-done
  29.8 0.1 fusion.20
  29.9 12.0 %all-reduce.1 = (f32[128]{0:T(128)S(1)}, f32[128]{0:T(128)S(1)}) all-reduce(f32[128]{0:T(128)S(1)} %get-tuple-element.13, f32[128]{0:T(128)S(1)} %get-tuple-element.12), channel_id=1, replica_groups=mesh['row'=4,'col'=4,'dp'=2] {'row'}, use_global_device_ids=true, to_apply=%region_3.4 | all-reduce | flops 256 | bytes 2048 | tf_op jit(solution)/shard_map/psum | solution.py:46
  41.9 0.9 fusion.25
  42.8 0.0 all-gather.7.cloned.1.call-update
  42.9 0.0 all-gather.5.cloned.1.call-start
  42.9 0.0 copy-done.1
  42.9 0.8 fusion.17
  43.7 0.0 all-gather.5.cloned.1.call-update
  43.7 0.0 reduce-scatter.9.cloned.1.call-start
  43.7 22.3 %all-gather.7.cloned.1.call-done = bf16[512,1024]{1,0:T(8,128)(2,1)} async-done(((bf16[128,1024]{1,0:T(8,128)(2,1)}), bf16[512,1024]{1,0:T(8,128)(2,1)}) %all-gather.7.cloned.1.call-update) | async-done | bytes 1048592 | tf_op jit(solution)/shard_map/all_gather | solution.py:52
  66.0 10.2 %convolution_convert_fusion.2 = bf16[512,4096]{1,0:T(8,128)(2,1)} fusion(bf16[512,1024]{1,0:T(8,128)(2,1)} %all-gather.7.cloned.1.call-done, bf16[1024,4096]{1,0:T(8,128)(2,1)} %param.9), kind=kOutput, calls=%fused_computation.2 | convolution fusion | flops 4297064448 | bytes 13631488 | tf_op jit(solution)/shard_map/dot_general | solution.py:55
  76.2 0.0 reduce-scatter.9.cloned.1.call-update
  76.3 0.0 reduce-scatter.7.cloned.1.call-start
  76.3 18.8 %all-gather.5.cloned.1.call-done = bf16[512,1024]{1,0:T(8,128)(2,1)} async-done(((bf16[128,1024]{1,0:T(8,128)(2,1)}), bf16[512,1024]{1,0:T(8,128)(2,1)}) %all-gather.5.cloned.1.call-update) | async-done | bytes 1048592 | tf_op jit(solution)/shard_map/all_gather | solution.py:72
  95.1 10.3 %convolution_convert_fusion.3 = bf16[512,4096]{1,0:T(8,128)(2,1)} fusion(bf16[512,1024]{1,0:T(8,128)(2,1)} %all-gather.5.cloned.1.call-done, bf16[4096,1024]{1,0:T(8,128)(2,1)} %param.10), kind=kOutput, calls=%fused_computation.3 | convolution fusion | flops 4297064448 | bytes 13631488 | tf_op jit(solution)/shard_map/dot_general | solution.py:80
  105.4 0.0 reduce-scatter.7.cloned.1.call-update
  105.4 0.0 all-gather.9.cloned.1.call-start
  105.4 69.3 %reduce-scatter.9.cloned.1.call-done = bf16[128,4096]{1,0:T(8,128)(2,1)} async-done(((bf16[512,4096]{1,0:T(8,128)(2,1)}), bf16[128,4096]{1,0:T(8,128)(2,1)}) %reduce-scatter.9.cloned.1.call-update) | async-done | bytes 1048592 | tf_op jit(solution)/shard_map/reduce_scatter | solution.py:54
  174.8 80.1 %reduce-scatter.7.cloned.1.call-done = bf16[128,4096]{1,0:T(8,128)(2,1)} async-done(((bf16[512,4096]{1,0:T(8,128)(2,1)}), bf16[128,4096]{1,0:T(8,128)(2,1)}) %reduce-scatter.7.cloned.1.call-update) | async-done | bytes 1048592 | tf_op jit(solution)/shard_map/reduce_scatter | solution.py:79
  254.9 4.4 fusion.7
  259.3 0.0 all-gather.9.cloned.1.call-update
  259.3 0.0 all-gather.11.cloned.1.call-start
  259.4 0.5 all-gather.11.cloned.1.call-update
  259.9 0.2 reduce-scatter.11.cloned.1.call-start
  260.1 80.6 %all-gather.9.cloned.1.call-done = bf16[512,4096]{1,0:T(8,128)(2,1)} async-done(((bf16[128,4096]{1,0:T(8,128)(2,1)}), bf16[512,4096]{1,0:T(8,128)(2,1)}) %all-gather.9.cloned.1.call-update) | async-done | bytes 4194320 | tf_op jit(solution)/shard_map/all_gather | solution.py:88
  340.7 10.1 %convolution_convert_fusion.5 = bf16[512,1024]{1,0:T(8,128)(2,1)} fusion(bf16[512,4096]{1,0:T(8,128)(2,1)} %all-gather.9.cloned.1.call-done, bf16[1024,4096]{1,0:T(8,128)(2,1)} %param.9), kind=kOutput, calls=%fused_computation.24 | convolution fusion | flops 4295491584 | bytes 13631488 | tf_op jit(solution)/shard_map/dot_general | solution.py:94
  350.9 0.0 reduce-scatter.11.cloned.1.call-update
  350.9 0.0 copy-start.2
  350.9 0.0 reduce-scatter.13.cloned.1.call-start
  351.0 71.1 %all-gather.11.cloned.1.call-done = bf16[512,4096]{1,0:T(8,128)(2,1)} async-done(((bf16[128,4096]{1,0:T(8,128)(2,1)}), bf16[512,4096]{1,0:T(8,128)(2,1)}) %all-gather.11.cloned.1.call-update) | async-done | bytes 4194320 | tf_op jit(solution)/shard_map/all_gather | solution.py:61
  422.1 10.1 %convolution_convert_fusion.4 = bf16[512,1024]{1,0:T(8,128)(2,1)} fusion(bf16[512,4096]{1,0:T(8,128)(2,1)} %all-gather.11.cloned.1.call-done, bf16[4096,1024]{1,0:T(8,128)(2,1)} %param.10), kind=kOutput, calls=%fused_computation.23 | convolution fusion | flops 4295491584 | bytes 13631488 | tf_op jit(solution)/shard_map/dot_general | solution.py:64
  432.2 0.0 reduce-scatter.13.cloned.1.call-update
  432.2 0.0 reduce-scatter.15.cloned.1.call-start
  432.2 0.0 copy-done.2
  432.3 9.0 %convolution_convert_fusion.1 = bf16[1024,4096]{1,0:T(8,128)(2,1)} fusion(bf16[512,1024]{1,0:T(8,128)(2,1)S(1)} %copy-done.2, bf16[512,4096]{1,0:T(8,128)(2,1)} %all-gather.9.cloned.1.call-done), kind=kOutput, calls=%fused_computation.1 | convolution fusion | flops 4299161600 | bytes 13631488 | tf_op jit(solution)/shard_map/dot_general | solution.py:89
  441.3 0.0 copy-start.3
  441.3 0.0 reduce-scatter.15.cloned.1.call-update
  441.3 0.0 reduce-scatter.17.cloned.1.call-start
  441.4 1.1 copy-done.3
  442.5 9.0 %convolution_convert_fusion = bf16[4096,1024]{1,0:T(8,128)(2,1)} fusion(bf16[512,4096]{1,0:T(8,128)(2,1)} %all-gather.11.cloned.1.call-done, bf16[512,1024]{1,0:T(8,128)(2,1)S(1)} %copy-done.3), kind=kOutput, calls=%fused_computation | convolution fusion | flops 4299161600 | bytes 13631488 | tf_op jit(solution)/shard_map/dot_general | solution.py:75
  451.5 0.0 reduce-scatter.17.cloned.1.call-update
  451.6 0.3 reduce-scatter.11.cloned.1.call-done
  451.8 1.2 fusion.26
  453.1 11.9 %all-reduce = (f32[128]{0:T(128)S(1)}, f32[128]{0:T(128)S(1)}) all-reduce(f32[128]{0:T(128)S(1)} %get-tuple-element.9, f32[128]{0:T(128)S(1)} %get-tuple-element.10), channel_id=1, replica_groups=mesh['row'=4,'col'=4,'dp'=2] {'row'}, use_global_device_ids=true, to_apply=%region_11.12 | all-reduce | flops 256 | bytes 2048 | tf_op jit(solution)/shard_map/psum | solution.py:110
  465.0 18.3 %reduce-scatter.13.cloned.1.call-done = bf16[128,1024]{1,0:T(8,128)(2,1)} async-done(((bf16[512,1024]{1,0:T(8,128)(2,1)}), bf16[128,1024]{1,0:T(8,128)(2,1)}) %reduce-scatter.13.cloned.1.call-update) | async-done | bytes 262160 | tf_op jit(solution)/shard_map/reduce_scatter | solution.py:63
  483.3 2.0 fusion.19
  485.4 0.1 multiply_convert_fusion
  485.5 23.1 %psum.47 = bf16[4,3,1024]{2,0,1:T(4,128)(2,1)S(1)} all-reduce(bf16[4,3,1024]{2,0,1:T(4,128)(2,1)S(1)} %multiply_convert_fusion), channel_id=1, replica_groups=mesh['row'=4,'col'=4,'dp'=2] {'col','dp'}, use_global_device_ids=true, to_apply=%region_16.17 | all-reduce | flops 12288 | bytes 49152 | tf_op jit(solution)/shard_map/psum | solution.py:121
  508.6 7.8 %convolution_bitcast_fusion = f32[3,1024,1024]{1,2,0:T(8,128)} fusion(bf16[4,3,1024]{2,0,1:T(4,128)(2,1)S(1)} %psum.47, s32[]{:T(128)S(6)} %select_n.7, f32[4,2048]{1,0:T(4,128)S(1)} %get-tuple-element.26, f32[4,2048]{1,0:T(4,128)S(1)} %get-tuple-element.25), kind=kOutput, calls=%fused_computation.11 | convolution fusion | flops 25190400 | bytes 12673028 | tf_op jit(solution)/shard_map/vi,vko->kio/dot_general | solution.py:122
  516.4 13.5 %copy.10 = f32[3,1024,1024]{2,1,0:T(8,128)} copy(f32[3,1024,1024]{1,2,0:T(8,128)} %convolution_bitcast_fusion) | data formatting | bytes 25165824
  529.9 0.0 reduce-scatter.15.cloned.1.call-done
  529.9 6.7 %convert_element_type.103 = f32[1024,2048]{1,0:T(8,128)} convert(bf16[1024,2048]{1,0:T(8,128)(2,1)} %reduce-scatter.15.cloned.1.call-done) | non-fusion elementwise | flops 2097152 | bytes 12582912 | tf_op jit(solution)/shard_map/convert_element_type | solution.py:104
  536.5 0.0 reduce-scatter.17.cloned.1.call-done
  536.5 6.6 %convert_element_type.105 = f32[2048,1024]{1,0:T(8,128)} convert(bf16[2048,1024]{1,0:T(8,128)(2,1)} %reduce-scatter.17.cloned.1.call-done) | non-fusion elementwise | flops 2097152 | bytes 12582912 | tf_op jit(solution)/shard_map/convert_element_type | solution.py:107
  (7 shorter events, 0.1 us)
Async XLA Ops:
  7.2 22.6 %copy-start = (bf16[128,1024]{1,0:T(8,128)(2,1)S(1)}, bf16[128,1024]{1,0:T(8,128)(2,1)}, u32[]{:S(2)}) copy-start(bf16[128,1024]{1,0:T(8,128)(2,1)} %param.6) | copy-start | bytes 786436
  7.2 35.7 %copy-start.1 = (bf16[128,1024]{1,0:T(8,128)(2,1)S(1)}, bf16[128,1024]{1,0:T(8,128)(2,1)}, u32[]{:S(2)}) copy-start(bf16[128,1024]{1,0:T(8,128)(2,1)} %param.11) | copy-start | bytes 786436
  7.2 58.8 %all-gather.7.cloned.1.call-start = ((), (), s32[]{:S(2)}) async-start(), calls=%async_computation.8 | async-start | bytes 1310720 | tf_op jit(solution)/shard_map/all_gather | solution.py:52
  42.9 52.2 %all-gather.5.cloned.1.call-start = ((), (), s32[]{:S(2)}) async-start(), calls=%async_computation.6 | async-start | bytes 1310720 | tf_op jit(solution)/shard_map/all_gather | solution.py:72
  43.7 131.1 %reduce-scatter.9.cloned.1.call-start = ((), (), s32[]{:S(2)}) async-start(), calls=%async_computation.9 | async-start | bytes 5242880 | tf_op jit(solution)/shard_map/reduce_scatter | solution.py:54
  76.3 178.6 %reduce-scatter.7.cloned.1.call-start = ((), (), s32[]{:S(2)}) async-start(), calls=%async_computation.7 | async-start | bytes 5242880 | tf_op jit(solution)/shard_map/reduce_scatter | solution.py:79
  105.4 235.4 %all-gather.9.cloned.1.call-start = ((), (), s32[]{:S(2)}) async-start(), calls=%async_computation.10 | async-start | bytes 5242880 | tf_op jit(solution)/shard_map/all_gather | solution.py:88
  259.3 162.7 %all-gather.11.cloned.1.call-start = ((), (), s32[]{:S(2)}) async-start(), calls=%async_computation.12 | async-start | bytes 5242880 | tf_op jit(solution)/shard_map/all_gather | solution.py:61
  259.9 191.9 %reduce-scatter.11.cloned.1.call-start = ((), (), s32[]{:S(2)}) async-start(), calls=%async_computation.11 | async-start | bytes 1310720 | tf_op jit(solution)/shard_map/reduce_scatter | solution.py:93
  350.9 81.3 %copy-start.2 = (bf16[512,1024]{1,0:T(8,128)(2,1)S(1)}, bf16[512,1024]{1,0:T(8,128)(2,1)}, u32[]{:S(2)}) copy-start(bf16[512,1024]{1,0:T(8,128)(2,1)} %all-gather.7.cloned.1.call-done) | copy-start | bytes 3145732
  350.9 132.4 %reduce-scatter.13.cloned.1.call-start = ((), (), s32[]{:S(2)}) async-start(), calls=%async_computation.13 | async-start | bytes 1310720 | tf_op jit(solution)/shard_map/reduce_scatter | solution.py:63
  432.2 97.7 %reduce-scatter.15.cloned.1.call-start = ((), (), s32[]{:S(2)}) async-start(), calls=%async_computation.14 | async-start | bytes 12582912 | tf_op jit(solution)/shard_map/reduce_scatter | solution.py:102
  441.3 1.2 copy-start.3
  441.3 95.2 %reduce-scatter.17.cloned.1.call-start = ((), (), s32[]{:S(2)}) async-start(), calls=%async_computation.15 | async-start | bytes 12582912 | tf_op jit(solution)/shard_map/reduce_scatter | solution.py:105
Sparse Core Ops, SparseCore 0:
  43.0 22.9 all-gather.6
  68.4 26.6 all-gather.4
  98.0 76.7 reduce-scatter.8
  177.6 77.2 reduce-scatter.6
  259.4 81.2 all-gather.8
  342.7 79.2 all-gather.10
  425.5 26.2 reduce-scatter.10
  455.5 27.7 reduce-scatter.12
  486.2 16.7 reduce-scatter.14
  505.3 18.0 reduce-scatter.16
where the time goes:
time: 551 us; the launch traced here: 550 us
  waiting for transfers between devices  361 us (66%)
  matrix products  70.4 us (13%)
  blocking collectives  64.7 us (12%)
  other arithmetic  24 us (4%)
  local copies, waits for them, and re-layouts  14.6 us (3%)
  between operations  14.3 us (3%)
    all_gather x1, waiting for transfers between devices, body(): grad_full = lax.all_gather(grad_hidden, 'row', axis=0, tiled=True)  80.6 us
    reduce_scatter x1, waiting for transfers between devices, body(): lax.psum_scatter(lax.dot_general(picked, down_weight, (((1,), (1,)), ((),...  80.1 us
    all_gather x1, waiting for transfers between devices, body(): act_full = lax.all_gather(act_own, 'row', axis=0, tiled=True)  71.1 us
    reduce_scatter x1, waiting for transfers between devices, body(): lax.psum_scatter(jnp.dot(picked, up_weight, preferred_element_type=jnp.fl...  69.3 us
    psum x1, blocking collectives, body(): lax.psum(placed.astype(jnp.bfloat16), ('col', 'dp')).astype(jnp.float32)  23.1 us
    all_gather x1, waiting for transfers between devices, body(): mod_full = lax.all_gather(modulated, 'col', axis=0, tiled=True)  22.3 us
    all_gather x1, waiting for transfers between devices, body(): branch_full = lax.all_gather(grad_branch, 'col', axis=0, tiled=True)  18.8 us
    reduce_scatter x1, waiting for transfers between devices, body(): lax.psum_scatter(jnp.dot(picked, down_weight, preferred_element_type=jnp....  18.3 us
  transfers between devices with their start and end apart: 10, of which 8 were waited for; matrix products, arithmetic and copies ran while one was open for 17% of the time, Pallas kernels for 0%

commit v1 on v0

v1 whole, which is shorter than its diff:
```python
import functools
import math

import jax
import jax.numpy as jnp
from jax import lax
from jax.experimental import pallas as pl
from jax.experimental.pallas import tpu as pltpu
from jax.sharding import PartitionSpec as P

MESH = pl.DeviceIdType.MESH
F32 = jnp.float32
BF16 = jnp.bfloat16
VMEM = pl.BlockSpec(memory_space=pltpu.VMEM)
MIB = 1 << 20
tanh_scale = math.sqrt(2.0 / math.pi)


def time_features(timesteps, width):
    half = width // 2
    freqs = jnp.exp(-math.log(10000.0) * jnp.arange(half, dtype=jnp.float32) / half)
    angles = timesteps.astype(jnp.float32)[:, None] * freqs[None, :]
    embed = jnp.concatenate([jnp.cos(angles), jnp.sin(angles)], axis=1)
    return jax.nn.silu(embed).astype(jnp.bfloat16)


def remote(src, dst, send, recv, device):
    return pltpu.make_async_remote_copy(
        src_ref=src, dst_ref=dst, send_sem=send, recv_sem=recv, device_id=device, device_id_type=MESH
    )


def greet(devices):
    barrier = pltpu.get_barrier_semaphore()
    for device in devices:
        pl.semaphore_signal(barrier, inc=1, device_id=device, device_id_type=MESH)
    pl.semaphore_wait(barrier, len(devices))


def others(axis, count):
    me = lax.axis_index(axis)
    return [lax.rem(me + step, count) for step in range(1, count)]


def token_columns(packed, square):
    square[...] = jnp.zeros_like(square)
    square[0:8, :] = packed
    turned = jnp.transpose(square[...])
    return turned[:, 0:1], turned[:, 4:5]


def token_stats(total, squares, full_width):
    mean = total / full_width
    var = squares / full_width - mean * mean
    return mean, lax.rsqrt(var + 1e-06)


def enter_kernel(
    rows, cols, full_width, tok, cot, terms, sums, full, mod_out, sums_out,
    got_terms, got_sums, square, send_terms, recv_terms, send_sums, recv_sums, send_full, recv_full,
):
    row, col = lax.axis_index("row"), lax.axis_index("col")
    row_peers, col_peers = others("row", rows), others("col", cols)
    greet([{"row": p} for p in row_peers] + [{"col": p} for p in col_peers])
    for at, p in enumerate(row_peers):
        remote(sums, got_sums.at[row], send_sums.at[at], recv_sums.at[row], {"row": p}).start()
    for at, p in enumerate(col_peers):
        remote(terms.at[p], got_terms.at[col], send_terms.at[at], recv_terms.at[col], {"col": p}).start()
    mod = terms[col]
    for at, p in enumerate(col_peers):
        remote(terms.at[p], got_terms.at[p], send_terms.at[at], recv_terms.at[p], {"col": p}).wait_recv()
        mod = mod + got_terms[p]
    packed = sums[...]
    for at, p in enumerate(row_peers):
        remote(sums, got_sums.at[p], send_sums.at[at], recv_sums.at[p], {"row": p}).wait_recv()
        packed = packed + got_sums[p]
    mod_out[...] = mod
    sums_out[...] = packed
    mean, rstd = token_stats(*token_columns(packed, square), full_width)
    normed = (tok[...].astype(F32) - mean) * rstd
    full[0, col] = (normed * (1.0 + mod[1:2]) + mod[0:1]).astype(BF16)
    full[1, col] = (cot[...].astype(F32) * mod[2:3]).astype(BF16)
    for at, p in enumerate(col_peers):
        remote(full.at[:, col], full.at[:, col], send_full.at[at], recv_full.at[col], {"col": p}).start()
    for at, p in enumerate(col_peers):
        remote(full.at[:, p], full.at[:, p], send_full.at[at], recv_full.at[p], {"col": p}).wait_recv()
    for at, p in enumerate(row_peers):
        remote(sums, got_sums.at[row], send_sums.at[at], recv_sums.at[row], {"row": p}).wait_send()
    for at, p in enumerate(col_peers):
        remote(terms.at[p], got_terms.at[col], send_terms.at[at], recv_terms.at[col], {"col": p}).wait_send()
        remote(full.at[:, col], full.at[:, col], send_full.at[at], recv_full.at[col], {"col": p}).wait_send()


def enter(rows, cols, full_width, tok, cot, terms, sums):
    n, width = tok.shape
    dma = pltpu.SemaphoreType.DMA
    return pl.pallas_call(
        functools.partial(enter_kernel, rows, cols, full_width),
        out_shape=(
            jax.ShapeDtypeStruct((2, cols, n, width), BF16),
            jax.ShapeDtypeStruct((8, width), F32),
            jax.ShapeDtypeStruct((8, n), F32),
        ),
        in_specs=[VMEM] * 4,
        out_specs=(VMEM,) * 3,
        scratch_shapes=[
            pltpu.VMEM((cols, 8, width), F32),
            pltpu.VMEM((rows, 8, n), F32),
            pltpu.VMEM((128, n), F32),
            dma((cols,)), dma((cols,)), dma((rows,)), dma((rows,)), dma((cols,)), dma((cols,)),
        ],
        compiler_params=pltpu.CompilerParams(
            collective_id=0, has_side_effects=True, vmem_limit_bytes=24 * MIB
        ),
        name="enter",
    )(tok, cot, terms, sums)


def middle_kernel(
    n, chunks, hid, gact, act, ghid, got_h, got_g,
    rs_send_r, rs_send_l, rs_recv, ag_send_r, ag_send_l, ag_recv,
):
    r = lax.axis_index("row")
    from_right = n - 1 - r
    block = hid.shape[0] // n
    wide = hid.shape[1] // chunks
    ins, gots, outs = (hid, gact), (got_h, got_g), (act, ghid)
    right, left = {"row": lax.rem(r + 1, n)}, {"row": lax.rem(r + n - 1, n)}
    inner_right, inner_left = r < n - 1, r > 0

    barrier = pltpu.get_barrier_semaphore()

    @pl.when(inner_right)
    def _():
        pl.semaphore_signal(barrier, inc=1, device_id=right, device_id_type=MESH)

    @pl.when(inner_left)
    def _():
        pl.semaphore_signal(barrier, inc=1, device_id=left, device_id_type=MESH)

    @pl.when(inner_right & inner_left)
    def _():
        pl.semaphore_wait(barrier, 2)

    @pl.when(jnp.logical_not(inner_right & inner_left))
    def _():
        pl.semaphore_wait(barrier, 1)

    def columns(k):
        return pl.ds(pl.multiple_of(k * wide, wide), wide)

    def rows(j):
        return pl.ds(pl.multiple_of(j * block, block), block)

    def sum_right(w, k, j, own):
        src = ins[w].at[rows(j), columns(k)] if own else gots[w].at[j, :, columns(k)]
        return remote(src, gots[w].at[j, :, columns(k)], rs_send_r.at[w, k, j], rs_recv.at[w, k, j], right)

    def sum_left(w, k, j, own):
        slot = jnp.where(j == r - 1, n, j)
        src = ins[w].at[rows(j), columns(k)] if own else gots[w].at[j, :, columns(k)]
        return remote(src, gots[w].at[slot, :, columns(k)], rs_send_l.at[w, k, j], rs_recv.at[w, k, slot], left)

    def arrived(w, k, slot):
        remote(
            gots[w].at[slot, :, columns(k)], gots[w].at[slot, :, columns(k)],
            rs_send_r.at[w, k, 0], rs_recv.at[w, k, slot], right,
        ).wait_recv()

    def pass_right(w, k, j):
        at = outs[w].at[rows(j), columns(k)]
        return remote(at, at, ag_send_r.at[w, k, j], ag_recv.at[w, k, j], right)

    def pass_left(w, k, j):
        at = outs[w].at[rows(j), columns(k)]
        return remote(at, at, ag_send_l.at[w, k, j], ag_recv.at[w, k, j], left)

    def begin(k):
        @pl.when(r == 0)
        def _():
            for t in range(n - 1):
                for w in range(2):
                    sum_right(w, k, n - 1 - t, True).start()

        @pl.when(from_right == 0)
        def _():
            for t in range(n - 1):
                for w in range(2):
                    sum_left(w, k, t, True).start()

    def add(w, k, j):
        own = ins[w][rows(j), columns(k)].astype(F32)
        gots[w][j, :, columns(k)] = (gots[w][j, :, columns(k)].astype(F32) + own).astype(BF16)

    def sum_step(k, t):
        @pl.when((r > 0) & (r <= t))
        def _():
            j = n - 1 - t + r
            for w in range(2):
                arrived(w, k, j)
                add(w, k, j)
                sum_right(w, k, j, False).start()

        @pl.when((from_right > 0) & (from_right <= t))
        def _():
            j = t - from_right
            for w in range(2):
                arrived(w, k, j)
                add(w, k, j)
                sum_left(w, k, j, False).start()

    def finish(k):
        for w in range(2):
            @pl.when(inner_left)
            def _():
                arrived(w, k, r)

            @pl.when(inner_right)
            def _():
                arrived(w, k, n)

        def total(w):
            own = ins[w][rows(r), columns(k)].astype(F32)
            one = gots[w][r, :, columns(k)].astype(F32)
            two = gots[w][n, :, columns(k)].astype(F32)
            return own + jnp.where(inner_left, one, 0.0) + jnp.where(inner_right, two, 0.0)

        h = total(0)
        g = total(1)
        inner = jnp.tanh(tanh_scale * (h + 0.044715 * h * h * h))
        act[rows(r), columns(k)] = (0.5 * h * (1.0 + inner)).astype(BF16)
        slope = 0.5 * (1.0 + inner) + 0.5 * h * (1.0 - inner * inner) * tanh_scale * (
            1.0 + 3.0 * 0.044715 * h * h
        )
        ghid[rows(r), columns(k)] = (g * slope).astype(BF16)

    def pass_step(k, t):
        @pl.when(t <= r)
        def _():
            j = r - t
            for w in range(2):
                if t > 0:
                    pass_right(w, k, j).wait_recv()

                @pl.when(inner_right)
                def _():
                    pass_right(w, k, j).start()

        @pl.when(t <= from_right)
        def _():
            j = r + t
            for w in range(2):
                if t > 0:
                    pass_left(w, k, j).wait_recv()

                @pl.when(inner_left)
                def _():
                    pass_left(w, k, j).start()

    @pl.when(r == 0)
    def _():
        for w in range(2):
            gots[w][0] = jnp.zeros(gots[w].shape[1:], BF16)

    @pl.when(from_right == 0)
    def _():
        for w in range(2):
            gots[w][n] = jnp.zeros(gots[w].shape[1:], BF16)

    begin(0)

    def chunk(k, carry):
        @pl.when(k > 0)
        def _():
            pass_step(k - 1, 0)

        @pl.when(k + 1 < chunks)
        def _():
            begin(k + 1)

        for t in range(1, n):
            if t < n - 1:
                @pl.when(k < chunks)
                def _():
                    sum_step(k, t)

            @pl.when(k > 0)
            def _():
                pass_step(k - 1, t)

        @pl.when(k < chunks)
        def _():
            finish(k)

        return carry

    lax.fori_loop(0, chunks + 1, chunk, 0)

    def drain(k, carry):
        for j in range(n):
            for w in range(2):
                @pl.when(j > r)
                def _():
                    sum_right(w, k, j, False).wait_send()

                @pl.when(j < r)
                def _():
                    sum_left(w, k, j, False).wait_send()

                @pl.when((j <= r) & inner_right)
                def _():
                    pass_right(w, k, j).wait_send()

                @pl.when((j >= r) & inner_left)
                def _():
                    pass_left(w, k, j).wait_send()

        return carry

    lax.fori_loop(0, chunks, drain, 0)


def middle(rows, chunks, hid, gact):
    tokens, width = hid.shape
    block = tokens // rows
    dma = pltpu.SemaphoreType.DMA
    whole = jax.ShapeDtypeStruct((tokens, width), BF16)
    return pl.pallas_call(
        functools.partial(middle_kernel, rows, chunks),
        out_shape=(whole, whole),
        in_specs=[VMEM] * 2,
        out_specs=(VMEM,) * 2,
        scratch_shapes=[
            pltpu.VMEM((rows + 1, block, width), BF16),
            pltpu.VMEM((rows + 1, block, width), BF16),
            dma((2, chunks, rows)), dma((2, chunks, rows)), dma((2, chunks, rows + 1)),
            dma((2, chunks, rows)), dma((2, chunks, rows)), dma((2, chunks, rows)),
        ],
        compiler_params=pltpu.CompilerParams(
            collective_id=1, has_side_effects=True, vmem_limit_bytes=48 * MIB
        ),
        name="middle",
    )(hid, gact)


def leave_kernel(
    rows, cols, dps, full_width, branch, gmod, tok, cot, mod, sums, grad_tok, grad_mod,
    got, own_mod, got_mod, own_sums, got_sums, square,
    send_got, recv_got, send_mod, recv_mod, send_sums, recv_sums,
):
    row, col, dp = lax.axis_index("row"), lax.axis_index("col"), lax.axis_index("dp")
    row_peers, col_peers = others("row", rows), others("col", cols)
    group = cols * dps
    me = col * dps + dp
    mod_peers = [lax.rem(me + step, group) for step in range(1, group)]
    place = lambda p: {"col": p // dps, "dp": lax.rem(p, dps)}
    greet([{"row": p} for p in row_peers] + [place(p) for p in mod_peers])
    parts = (branch, gmod)
    for at, p in enumerate(col_peers):
        for w in range(2):
            remote(parts[w].at[p], got.at[w, col], send_got.at[w, at], recv_got.at[w, col], {"col": p}).start()
    mean, rstd = token_stats(*token_columns(sums[...], square), full_width)
    normed = (tok[...].astype(F32) - mean) * rstd
    cotf = cot[...].astype(F32)
    summed = []
    for w in range(2):
        total = parts[w][col].astype(F32)
        for at, p in enumerate(col_peers):
            remote(parts[w].at[p], got.at[w, p], send_got.at[w, at], recv_got.at[w, p], {"col": p}).wait_recv()
            total = total + got[w, p].astype(F32)
        summed.append(total)
    grad_norm = summed[1] * (1.0 + mod[1:2])
    lane = lax.broadcasted_iota(jnp.int32, square.shape, 1)
    one = jnp.sum(grad_norm, axis=1, keepdims=True)
    two = jnp.sum(grad_norm * normed, axis=1, keepdims=True)
    own_sums[...] = jnp.transpose(jnp.where(lane < 4, one, two))[0:8, :]
    for at, p in enumerate(row_peers):
        remote(own_sums, got_sums.at[row], send_sums.at[at], recv_sums.at[row], {"row": p}).start()
    own_mod[...] = jnp.zeros_like(own_mod)
    own_mod[0:1] = jnp.sum(summed[1], axis=0, keepdims=True)
    own_mod[1:2] = jnp.sum(summed[1] * normed, axis=0, keepdims=True)
    own_mod[2:3] = jnp.sum(cotf * summed[0], axis=0, keepdims=True)
    for at, p in enumerate(mod_peers):
        remote(own_mod, got_mod.at[me], send_mod.at[at], recv_mod.at[me], place(p)).start()
    packed = own_sums[...]
    for at, p in enumerate(row_peers):
        remote(own_sums, got_sums.at[p], send_sums.at[at], recv_sums.at[p], {"row": p}).wait_recv()
        packed = packed + got_sums[p]
    first, second = token_columns(packed, square)
    first = first / full_width
    second = second / full_width
    grad_tok[...] = (cotf + rstd * (grad_norm - first - normed * second)).astype(BF16)
    got_mod[me] = own_mod[...]
    for at, p in enumerate(mod_peers):
        remote(own_mod, got_mod.at[p], send_mod.at[at], recv_mod.at[p], place(p)).wait_recv()
    for v in range(cols):
        total = got_mod[v * dps]
        for d in range(1, dps):
            total = total + got_mod[v * dps + d]
        grad_mod[v] = total
    for at, p in enumerate(col_peers):
        for w in range(2):
            remote(parts[w].at[p], got.at[w, col], send_got.at[w, at], recv_got.at[w, col], {"col": p}).wait_send()
    for at, p in enumerate(row_peers):
        remote(own_sums, got_sums.at[row], send_sums.at[at], recv_sums.at[row], {"row": p}).wait_send()
    for at, p in enumerate(mod_peers):
        remote(own_mod, got_mod.at[me], send_mod.at[at], recv_mod.at[me], place(p)).wait_send()


def leave(rows, cols, dps, full_width, branch, gmod, tok, cot, mod, sums):
    n, width = tok.shape
    dma = pltpu.SemaphoreType.DMA
    group = cols * dps
    return pl.pallas_call(
        functools.partial(leave_kernel, rows, cols, dps, full_width),
        out_shape=(
            jax.ShapeDtypeStruct((n, width), BF16),
            jax.ShapeDtypeStruct((cols, 8, width), F32),
        ),
        in_specs=[VMEM] * 6,
        out_specs=(VMEM,) * 2,
        scratch_shapes=[
            pltpu.VMEM((2, cols, n, width), BF16),
            pltpu.VMEM((8, width), F32),
            pltpu.VMEM((group, 8, width), F32),
            pltpu.VMEM((8, n), F32),
            pltpu.VMEM((rows, 8, n), F32),
            pltpu.VMEM((128, n), F32),
            dma((2, cols)), dma((2, cols)), dma((group,)), dma((group,)), dma((rows,)), dma((rows,)),
        ],
        compiler_params=pltpu.CompilerParams(
            collective_id=2, has_side_effects=True, vmem_limit_bytes=24 * MIB
        ),
        name="leave",
    )(branch, gmod, tok, cot, mod, sums)


def body(tokens, timesteps, ada_weight, up_weight, down_weight, cotangent):
    rows = lax.axis_size("row")
    cols = lax.axis_size("col")
    dps = lax.axis_size("dp")
    n, width = tokens.shape
    full_width = width * rows
    in_width = ada_weight.shape[1]
    cond = time_features(timesteps, full_width)
    cond_part = lax.dynamic_slice_in_dim(cond, lax.axis_index("col") * in_width, in_width, 1)
    terms = jnp.einsum("vi,kio->vko", cond_part, ada_weight, preferred_element_type=F32)
    terms = jnp.pad(terms, ((0, 0), (0, 5), (0, 0)))
    x = tokens.astype(F32)
    total = jnp.sum(x, axis=1)
    squares = jnp.sum(x * x, axis=1)
    sums = jnp.stack([total] * 4 + [squares] * 4, axis=0)
    full, mod, sums = enter(rows, cols, full_width, tokens, cotangent, terms, sums)
    mod_full = full[0].reshape(cols * n, width)
    grad_full = full[1].reshape(cols * n, width)
    hid = jnp.dot(mod_full, up_weight, preferred_element_type=F32).astype(BF16)
    gact = lax.dot_general(
        grad_full, down_weight, (((1,), (1,)), ((), ())), preferred_element_type=F32
    ).astype(BF16)
    act, ghid = middle(rows, 8, hid, gact)
    branch = jnp.dot(act, down_weight, preferred_element_type=F32).astype(BF16)
    gmod = lax.dot_general(
        ghid, up_weight, (((1,), (1,)), ((), ())), preferred_element_type=F32
    ).astype(BF16)
    down_part = lax.dot_general(
        act, grad_full, (((0,), (0,)), ((), ())), preferred_element_type=F32
    )
    up_part = lax.dot_general(
        mod_full, ghid, (((0,), (0,)), ((), ())), preferred_element_type=F32
    )
    grad_up = lax.psum_scatter(
        up_part.astype(BF16), "dp", scatter_dimension=1, tiled=True
    ).astype(F32)
    grad_down = lax.psum_scatter(
        down_part.astype(BF16), "dp", scatter_dimension=0, tiled=True
    ).astype(F32)
    grad_tokens, grad_mod = leave(
        rows, cols, dps, full_width,
        branch.reshape(cols, n, width), gmod.reshape(cols, n, width), tokens, cotangent, mod, sums,
    )
    grad_ada = jnp.einsum(
        "vi,vko->kio", cond_part.astype(F32), grad_mod[:, :3], precision=lax.Precision.HIGHEST
    )
    return (grad_tokens, grad_ada, grad_up, grad_down)


def solution(mesh):
    return jax.shard_map(
        body,
        mesh=mesh,
        in_specs=(
            P(("col", "dp"), "row"),
            P(),
            P(None, "col", "row"),
            P("row", "col"),
            P("col", "row"),
            P(("col", "dp"), "row"),
        ),
        out_specs=(
            P(("col", "dp"), "row"),
            P(None, "col", "row"),
            P("row", ("col", "dp")),
            P(("col", "dp"), "row"),
        ),
        check_vma=False,
    )
```

time: 551 us -> 399 us (0.72)
  waiting for transfers between devices: 361 us -> 0.04 us
  Pallas kernels: 0 us -> 287 us
  blocking collectives: 64.7 us -> 0 us
  other arithmetic: 24 us -> 14.5 us
    pallas_call x0 -> x3, Pallas kernels: none -> 287 us  [the longest x1 222 us: middle(): pl.pallas_call(functools.partial(middle_kernel, rows, chunks), out_shape=...]
    all_gather x4 -> x0, waiting for transfers between devices: 193 us -> none  [the longest x1 80.6 us: body(): grad_full = lax.all_gather(grad_hidden, 'row', axis=0, tiled=True)]
    reduce_scatter x6 -> x2, waiting for transfers between devices: 168 us -> 0.01 us  [the longest x1 0.01 us: body(): lax.psum_scatter(up_part.astype(BF16), 'dp', scatter_dimension=1, tiled=T...]
    psum x4 -> x0, blocking collectives: 64.7 us -> none  [the longest x1 23.1 us: body(): lax.psum(placed.astype(jnp.bfloat16), ('col', 'dp')).astype(jnp.float32)]
    convert_element_type x8 -> x2, other arithmetic: 19.5 us -> 13.3 us  [the longest x1 6.65 us: body(): grad_up = lax.psum_scatter(up_part.astype(BF16), 'dp', scatter_dimension=...]
    unnamed x9 -> x10, local copies, waits for them, and re-layouts: 14.6 us -> 15.3 us
  transfers between devices with their start and end apart: 10 -> 2, of which waited for: 8 -> 0; matrix products, arithmetic and copies ran while one was open for 17% -> 14% of each run, Pallas kernels for 0% -> 8%
where the time goes in v1:
time: 399 us
  Pallas kernels  287 us (72%)
  matrix products  67.3 us (17%)
  local copies, waits for them, and re-layouts  15.6 us (4%)
  other arithmetic  14.5 us (4%)
  between operations  14.2 us (4%)
    pallas_call x1, Pallas kernels, middle(): pl.pallas_call(functools.partial(middle_kernel, rows, chunks), out_shape=...  222 us
    pallas_call x1, Pallas kernels, enter(): pl.pallas_call(functools.partial(enter_kernel, rows, cols, full_width), o...  32.9 us
    pallas_call x1, Pallas kernels, leave(): pl.pallas_call(functools.partial(leave_kernel, rows, cols, dps, full_widt...  31.6 us
    unnamed x10, local copies, waits for them, and re-layouts  15.3 us
    dot_general x1, matrix products, body(): branch = jnp.dot(act, down_weight, preferred_element_type=F32).astype(BF16)  11 us
    dot_general x1, matrix products, body(): lax.dot_general(grad_full, down_weight, (((1,), (1,)), ((), ())), preferr...  9.56 us
    dot_general x1, matrix products, body(): lax.dot_general(act, grad_full, (((0,), (0,)), ((), ())), preferred_eleme...  9.53 us
    dot_general x1, matrix products, body(): hid = jnp.dot(mod_full, up_weight, preferred_element_type=F32).astype(BF16)  9.41 us
  transfers between devices with their start and end apart: 2, of which 0 were waited for; matrix products, arithmetic and copies ran while one was open for 14% of the time, Pallas kernels for 8%

profile of v1, /device:TPU:0, one launch (start us, length us, event | category | flops | bytes accessed | tf_op | source)
XLA Modules:
  0.0 398.8 jit_solution(7495742561829594052)
XLA Ops:
  7.2 0.0 copy-start
  7.2 0.0 copy-start.1
  7.2 0.0 reduce-scatter.3.cloned.1.call-start
  7.3 0.7 convert_element_type.36
  8.0 0.3 multiply_cosine_fusion
  8.3 3.7 fusion.5
  12.0 0.0 copy-done
  12.1 0.1 fusion
  12.2 0.0 copy-done.1
  12.3 32.9 %enter.1 = (bf16[2,4,128,1024]{3,2,1,0:T(8,128)(2,1)S(1)}, f32[8,1024]{1,0:T(8,128)S(1)}, f32[8,128]{1,0:T(8,128)S(1)}) custom-call(bf16[128,1024]{1,0:T(8,128)(2,1)S(1)} %copy-done, bf16[128,1024]{1,0:T(8,128)(2,1)S(1)} %copy-done.1, f32[4,8,1024]{2,1,0:T(8,128)S(1)} %pad.4.terms, f32[8,128]{1,0:T(8,128)S(1)} %stack.8.sums), custom_call_target="tpu_custom_call" | custom-call | tf_op jit(solution)/shard_map/enter/pallas_call | solution.py:97
  45.2 0.2 fusion.9
  45.4 9.4 %convolution_convert_fusion.3.hid = bf16[512,4096]{1,0:T(8,128)(2,1)} fusion(bf16[512,1024]{1,0:T(8,128)(2,1)S(1)} %bitcast.30, bf16[1024,4096]{1,0:T(8,128)(2,1)} %param.9), kind=kOutput, calls=%fused_computation.3 | convolution fusion | flops 4297064448 | bytes 13631488 | tf_op jit(solution)/shard_map/dot_general | solution.py:456
  54.8 9.6 %convolution_convert_fusion.2.gact = bf16[512,4096]{1,0:T(8,128)(2,1)} fusion(bf16[512,1024]{1,0:T(8,128)(2,1)S(1)} %bitcast.28, bf16[4096,1024]{1,0:T(8,128)(2,1)} %param.10), kind=kOutput, calls=%fused_computation.2 | convolution fusion | flops 4297064448 | bytes 13631488 | tf_op jit(solution)/shard_map/dot_general | solution.py:457
  64.4 222.4 %middle.1 = (bf16[512,4096]{1,0:T(8,128)(2,1)S(1)}, bf16[512,4096]{1,0:T(8,128)(2,1)}) custom-call(bf16[512,4096]{1,0:T(8,128)(2,1)} %convolution_convert_fusion.3.hid, bf16[512,4096]{1,0:T(8,128)(2,1)} %convolution_convert_fusion.2.gact), custom_call_target="tpu_custom_call" | custom-call | tf_op jit(solution)/shard_map/middle/pallas_call | solution.py:328
  286.8 0.0 copy-start.2
  286.8 2.0 copy-done.2
  288.8 9.0 %convolution_convert_fusion.1 = bf16[1024,4096]{1,0:T(8,128)(2,1)} fusion(bf16[512,1024]{1,0:T(8,128)(2,1)S(1)} %bitcast.31, bf16[512,4096]{1,0:T(8,128)(2,1)} %get-tuple-element.13), kind=kOutput, calls=%fused_computation.1 | convolution fusion | flops 4299161600 | bytes 13631488 | tf_op jit(solution)/shard_map/dot_general | solution.py:468
  297.8 0.0 reduce-scatter.3.cloned.1.call-update
  297.8 0.2 reduce-scatter.5.cloned.1.call-start
  298.1 9.5 %convolution_convert_fusion = bf16[4096,1024]{1,0:T(8,128)(2,1)} fusion(bf16[512,4096]{1,0:T(8,128)(2,1)} %copy-done.2, bf16[512,1024]{1,0:T(8,128)(2,1)S(1)} %bitcast.29), kind=kOutput, calls=%fused_computation | convolution fusion | flops 4299161600 | bytes 13631488 | tf_op jit(solution)/shard_map/dot_general | solution.py:465
  307.6 0.0 reduce-scatter.5.cloned.1.call-update
  307.6 0.0 copy-start.3
  307.6 11.0 %convolution_convert_fusion.5 = bf16[512,1024]{1,0:T(8,128)(2,1)S(1)} fusion(bf16[512,4096]{1,0:T(8,128)(2,1)} %copy-done.2, bf16[4096,1024]{1,0:T(8,128)(2,1)} %param.10), kind=kOutput, calls=%fused_computation.6 | convolution fusion | flops 4295491584 | bytes 13631488 | tf_op jit(solution)/shard_map/dot_general | solution.py:461
  318.6 0.0 copy-done.3
  318.6 7.1 %convolution_convert_fusion.4 = bf16[512,1024]{1,0:T(8,128)(2,1)S(1)} fusion(bf16[512,4096]{1,0:T(8,128)(2,1)S(1)} %copy-done.3, bf16[1024,4096]{1,0:T(8,128)(2,1)} %param.9), kind=kOutput, calls=%fused_computation.5 | convolution fusion | flops 4295491584 | bytes 13631488 | tf_op jit(solution)/shard_map/dot_general | solution.py:462
  325.7 31.6 %leave.1 = (bf16[128,1024]{1,0:T(8,128)(2,1)S(1)}, f32[4,8,1024]{2,1,0:T(8,128)S(1)}) custom-call(bf16[4,128,1024]{2,1,0:T(8,128)(2,1)S(1)} %bitcast.26, bf16[4,128,1024]{2,1,0:T(8,128)(2,1)S(1)} %bitcast.27, bf16[128,1024]{1,0:T(8,128)(2,1)S(1)} %copy-done, bf16[128,1024]{1,0:T(8,128)(2,1)S(1)} %copy-done.1, f32[8,1024]{1,0:T(8,128)S(1)} %get-tuple-element.14.mod, ...), custom_call_target="tpu_custom_call" | custom-call | tf_op jit(solution)/shard_map/leave/pallas_call | solution.py:414
  357.3 8.0 %convolution_bitcast_fusion = f32[3,1024,1024]{1,2,0:T(8,128)} fusion(f32[4,3,1024]{2,1,0:T(4,128)S(1)} %slice.11, s32[]{:T(128)S(6)} %select_n.3, f32[4,2048]{1,0:T(4,128)S(1)} %get-tuple-element.27, f32[4,2048]{1,0:T(4,128)S(1)} %get-tuple-element.26), kind=kOutput, calls=%fused_computation.4 | convolution fusion | flops 151019520 | bytes 12697604 | tf_op jit(solution)/shard_map/vi,vko->kio/dot_general | solution.py:481
  365.3 12.6 %copy.12 = f32[3,1024,1024]{2,1,0:T(8,128)} copy(f32[3,1024,1024]{1,2,0:T(8,128)} %convolution_bitcast_fusion) | data formatting | bytes 25165824
  377.9 0.0 reduce-scatter.3.cloned.1.call-done
  377.9 6.7 %convert_element_type.44 = f32[1024,2048]{1,0:T(8,128)} convert(bf16[1024,2048]{1,0:T(8,128)(2,1)} %reduce-scatter.3.cloned.1.call-done) | non-fusion elementwise | flops 2097152 | bytes 12582912 | tf_op jit(solution)/shard_map/convert_element_type | solution.py:473
  384.6 0.0 reduce-scatter.5.cloned.1.call-done
  384.6 6.6 %convert_element_type.46 = f32[2048,1024]{1,0:T(8,128)} convert(bf16[2048,1024]{1,0:T(8,128)(2,1)} %reduce-scatter.5.cloned.1.call-done) | non-fusion elementwise | flops 2097152 | bytes 12582912 | tf_op jit(solution)/shard_map/convert_element_type | solution.py:476
  391.2 0.7 copy.16
  (5 shorter events, 0.1 us)
Async XLA Ops:
  7.2 4.9 %copy-start = (bf16[128,1024]{1,0:T(8,128)(2,1)S(1)}, bf16[128,1024]{1,0:T(8,128)(2,1)}, u32[]{:S(2)}) copy-start(bf16[128,1024]{1,0:T(8,128)(2,1)} %tok.3) | copy-start | bytes 786436
  7.2 5.1 %copy-start.1 = (bf16[128,1024]{1,0:T(8,128)(2,1)S(1)}, bf16[128,1024]{1,0:T(8,128)(2,1)}, u32[]{:S(2)}) copy-start(bf16[128,1024]{1,0:T(8,128)(2,1)} %cot.3) | copy-start | bytes 786436
  7.2 370.7 %reduce-scatter.3.cloned.1.call-start = ((), (), s32[]{:S(2)}) async-start(), calls=%async_computation.2 | async-start | bytes 12582912 | tf_op jit(solution)/shard_map/reduce_scatter | solution.py:471
  286.8 2.0 copy-start.2
  297.8 86.8 %reduce-scatter.5.cloned.1.call-start = ((), (), s32[]{:S(2)}) async-start(), calls=%async_computation.3 | async-start | bytes 12582912 | tf_op jit(solution)/shard_map/reduce_scatter | solution.py:474
  307.6 11.0 %copy-start.3 = (bf16[512,4096]{1,0:T(8,128)(2,1)S(1)}, bf16[512,4096]{1,0:T(8,128)(2,1)}, u32[]{:S(2)}) copy-start(bf16[512,4096]{1,0:T(8,128)(2,1)} %get-tuple-element.13) | copy-start | bytes 12582916
Sparse Core Ops, SparseCore 0:
  297.9 15.2 reduce-scatter.2
  315.6 18.0 reduce-scatter.4

commit v2 on v1

--- a/solution.py
+++ b/solution.py
@@ -117,8 +117,8 @@
 
 
 def middle_kernel(
-    n, chunks, hid, gact, act, ghid, got_h, got_g,
-    rs_send_r, rs_send_l, rs_recv, ag_send_r, ag_send_l, ag_recv,
+    n, chunks, mod_full, grad_full, up, down, act, ghid, hid, gact, up_in, down_in, got_h, got_g,
+    load_up, load_down, rs_send_r, rs_send_l, rs_recv, ag_send_r, ag_send_l, ag_recv,
 ):
     r = lax.axis_index("row")
     from_right = n - 1 - r
@@ -128,6 +128,17 @@
     right, left = {"row": lax.rem(r + 1, n)}, {"row": lax.rem(r + n - 1, n)}
     inner_right, inner_left = r < n - 1, r > 0
 
+    for k in range(chunks):
+        for load in (
+            pltpu.make_async_copy(
+                up.at[:, k * wide:(k + 1) * wide], up_in.at[:, k * wide:(k + 1) * wide], load_up.at[k]
+            ),
+            pltpu.make_async_copy(
+                down.at[k * wide:(k + 1) * wide], down_in.at[k * wide:(k + 1) * wide], load_down.at[k]
+            ),
+        ):
+            load.start()
+
     barrier = pltpu.get_barrier_semaphore()
 
     @pl.when(inner_right)
@@ -151,6 +162,22 @@
 
     def rows(j):
         return pl.ds(pl.multiple_of(j * block, block), block)
+
+    def loads(k):
+        return (
+            pltpu.make_async_copy(up.at[:, columns(k)], up_in.at[:, columns(k)], load_up.at[k]),
+            pltpu.make_async_copy(down.at[columns(k)], down_in.at[columns(k)], load_down.at[k]),
+        )
+
+    def multiply(k):
+        for load in loads(k):
+            load.wait()
+        hid[:, columns(k)] = jnp.dot(
+            mod_full[...], up_in[:, columns(k)], preferred_element_type=F32
+        ).astype(BF16)
+        gact[:, columns(k)] = lax.dot_general(
+            grad_full[...], down_in[columns(k)], (((1,), (1,)), ((), ())), preferred_element_type=F32
+        ).astype(BF16)
 
     def sum_right(w, k, j, own):
         src = ins[w].at[rows(j), columns(k)] if own else gots[w].at[j, :, columns(k)]
@@ -267,6 +294,7 @@
         for w in range(2):
             gots[w][n] = jnp.zeros(gots[w].shape[1:], BF16)
 
+    multiply(0)
     begin(0)
 
     def chunk(k, carry):
@@ -276,6 +304,7 @@
 
         @pl.when(k + 1 < chunks)
         def _():
+            multiply(k + 1)
             begin(k + 1)
 
         for t in range(1, n):
@@ -320,55 +349,49 @@
     lax.fori_loop(0, chunks, drain, 0)
 
 
-def middle(rows, chunks, hid, gact):
-    tokens, width = hid.shape
+def middle(rows, chunks, mod_full, grad_full, up, down):
+    tokens, width = mod_full.shape[0], up.shape[1]
     block = tokens // rows
     dma = pltpu.SemaphoreType.DMA
     whole = jax.ShapeDtypeStruct((tokens, width), BF16)
     return pl.pallas_call(
         functools.partial(middle_kernel, rows, chunks),
         out_shape=(whole, whole),
-        in_specs=[VMEM] * 2,
+        in_specs=[VMEM] * 2 + [pl.BlockSpec(memory_space=pl.ANY)] * 2,
         out_specs=(VMEM,) * 2,
         scratch_shapes=[
+            pltpu.VMEM((tokens, width), BF16),
+            pltpu.VMEM((tokens, width), BF16),
+            pltpu.VMEM(up.shape, BF16),
+            pltpu.VMEM(down.shape, BF16),
             pltpu.VMEM((rows + 1, block, width), BF16),
             pltpu.VMEM((rows + 1, block, width), BF16),
+            dma((chunks,)), dma((chunks,)),
             dma((2, chunks, rows)), dma((2, chunks, rows)), dma((2, chunks, rows + 1)),
             dma((2, chunks, rows)), dma((2, chunks, rows)), dma((2, chunks, rows)),
         ],
         compiler_params=pltpu.CompilerParams(
-            collective_id=1, has_side_effects=True, vmem_limit_bytes=48 * MIB
+            collective_id=1, has_side_effects=True, vmem_limit_bytes=56 * MIB
         ),
         name="middle",
-    )(hid, gact)
+    )(mod_full, grad_full, up, down)
 
 
 def leave_kernel(
-    rows, cols, dps, full_width, branch, gmod, tok, cot, mod, sums, grad_tok, grad_mod,
-    got, own_mod, got_mod, own_sums, got_sums, square,
-    send_got, recv_got, send_mod, recv_mod, send_sums, recv_sums,
+    rows, cols, dps, full_width, summed, tok, cot, mod, sums, grad_tok, grad_mod,
+    own_mod, got_mod, own_sums, got_sums, square,
+    send_mod, recv_mod, send_sums, recv_sums,
 ):
     row, col, dp = lax.axis_index("row"), lax.axis_index("col"), lax.axis_index("dp")
-    row_peers, col_peers = others("row", rows), others("col", cols)
+    row_peers = others("row", rows)
     group = cols * dps
     me = col * dps + dp
     mod_peers = [lax.rem(me + step, group) for step in range(1, group)]
     place = lambda p: {"col": p // dps, "dp": lax.rem(p, dps)}
     greet([{"row": p} for p in row_peers] + [place(p) for p in mod_peers])
-    parts = (branch, gmod)
-    for at, p in enumerate(col_peers):
-        for w in range(2):
-            remote(parts[w].at[p], got.at[w, col], send_got.at[w, at], recv_got.at[w, col], {"col": p}).start()
     mean, rstd = token_stats(*token_columns(sums[...], square), full_width)
     normed = (tok[...].astype(F32) - mean) * rstd
     cotf = cot[...].astype(F32)
-    summed = []
-    for w in range(2):
-        total = parts[w][col].astype(F32)
-        for at, p in enumerate(col_peers):
-            remote(parts[w].at[p], got.at[w, p], send_got.at[w, at], recv_got.at[w, p], {"col": p}).wait_recv()
-            total = total + got[w, p].astype(F32)
-        summed.append(total)
     grad_norm = summed[1] * (1.0 + mod[1:2])
     lane = lax.broadcasted_iota(jnp.int32, square.shape, 1)
     one = jnp.sum(grad_norm, axis=1, keepdims=True)
@@ -398,16 +421,13 @@
         for d in range(1, dps):
             total = total + got_mod[v * dps + d]
         grad_mod[v] = total
-    for at, p in enumerate(col_peers):
-        for w in range(2):
-            remote(parts[w].at[p], got.at[w, col], send_got.at[w, at], recv_got.at[w, col], {"col": p}).wait_send()
     for at, p in enumerate(row_peers):
         remote(own_sums, got_sums.at[row], send_sums.at[at], recv_sums.at[row], {"row": p}).wait_send()
     for at, p in enumerate(mod_peers):
         remote(own_mod, got_mod.at[me], send_mod.at[at], recv_mod.at[me], place(p)).wait_send()
 
 
-def leave(rows, cols, dps, full_width, branch, gmod, tok, cot, mod, sums):
+def leave(rows, cols, dps, full_width, summed, tok, cot, mod, sums):
     n, width = tok.shape
     dma = pltpu.SemaphoreType.DMA
     group = cols * dps
@@ -417,22 +437,21 @@
             jax.ShapeDtypeStruct((n, width), BF16),
             jax.ShapeDtypeStruct((cols, 8, width), F32),
         ),
-        in_specs=[VMEM] * 6,
+        in_specs=[VMEM] * 5,
         out_specs=(VMEM,) * 2,
         scratch_shapes=[
-            pltpu.VMEM((2, cols, n, width), BF16),
             pltpu.VMEM((8, width), F32),
             pltpu.VMEM((group, 8, width), F32),
             pltpu.VMEM((8, n), F32),
             pltpu.VMEM((rows, 8, n), F32),
             pltpu.VMEM((128, n), F32),
-            dma((2, cols)), dma((2, cols)), dma((group,)), dma((group,)), dma((rows,)), dma((rows,)),
+            dma((group,)), dma((group,)), dma((rows,)), dma((rows,)),
         ],
         compiler_params=pltpu.CompilerParams(
             collective_id=2, has_side_effects=True, vmem_limit_bytes=24 * MIB
         ),
         name="leave",
-    )(branch, gmod, tok, cot, mod, sums)
+    )(summed, tok, cot, mod, sums)
 
 
 def body(tokens, timesteps, ada_weight, up_weight, down_weight, cotangent):
@@ -453,34 +472,54 @@
     full, mod, sums = enter(rows, cols, full_width, tokens, cotangent, terms, sums)
     mod_full = full[0].reshape(cols * n, width)
     grad_full = full[1].reshape(cols * n, width)
-    hid = jnp.dot(mod_full, up_weight, preferred_element_type=F32).astype(BF16)
-    gact = lax.dot_general(
-        grad_full, down_weight, (((1,), (1,)), ((), ())), preferred_element_type=F32
-    ).astype(BF16)
-    act, ghid = middle(rows, 8, hid, gact)
+    act, ghid = middle(rows, 8, mod_full, grad_full, up_weight, down_weight)
     branch = jnp.dot(act, down_weight, preferred_element_type=F32).astype(BF16)
     gmod = lax.dot_general(
         ghid, up_weight, (((1,), (1,)), ((), ())), preferred_element_type=F32
     ).astype(BF16)
-    down_part = lax.dot_general(
-        act, grad_full, (((0,), (0,)), ((), ())), preferred_element_type=F32
+    col, dp = lax.axis_index("col"), lax.axis_index("dp")
+
+    def block_of(c):
+        return jnp.stack([lax.dynamic_slice_in_dim(a, c * n, n, 0) for a in (branch, gmod)])
+
+    blocks = [block_of((col + step) % cols) for step in range(cols)]
+    act, ghid, blocks = lax.optimization_barrier((act, ghid, blocks))
+    arrived = [blocks[0]]
+    for step in range(1, cols):
+        pairs = [(c, (c + step) % cols) for c in range(cols)]
+        arrived.append(lax.ppermute(blocks[step], "col", pairs))
+
+    half = act.shape[1] // dps
+
+    def down_part(d):
+        mine = lax.dynamic_slice_in_dim(act, d * half, half, 1)
+        return lax.dot_general(mine, grad_full, (((0,), (0,)), ((), ())), preferred_element_type=F32)
+
+    def up_part(d):
+        mine = lax.dynamic_slice_in_dim(ghid, d * half, half, 1)
+        return lax.dot_general(mod_full, mine, (((0,), (0,)), ((), ())), preferred_element_type=F32)
+
+    grads = []
+    for part in (down_part, up_part):
+        got = []
+        for step in range(1, dps):
+            pairs = [(d, (d + step) % dps) for d in range(dps)]
+            got.append(lax.ppermute(part((dp + step) % dps).astype(BF16), "dp", pairs))
+        total = part(dp)
+        for g in got:
+            total = total + g.astype(F32)
+        grads.append(total)
+    arrived, (grad_down, grad_up) = lax.optimization_barrier((arrived, grads))
+    summed = arrived[0].astype(F32)
+    for a in arrived[1:]:
+        summed = summed + a.astype(F32)
+    grad_tokens, grad_mod = leave(
+        rows, cols, dps, full_width, summed, tokens, cotangent, mod, sums
     )
-    up_part = lax.dot_general(
-        mod_full, ghid, (((0,), (0,)), ((), ())), preferred_element_type=F32
-    )
-    grad_up = lax.psum_scatter(
-        up_part.astype(BF16), "dp", scatter_dimension=1, tiled=True
-    ).astype(F32)
-    grad_down = lax.psum_scatter(
-        down_part.astype(BF16), "dp", scatter_dimension=0, tiled=True
-    ).astype(F32)
-    grad_tokens, grad_mod = leave(
-        rows, cols, dps, full_width,
-        branch.reshape(cols, n, width), gmod.reshape(cols, n, width), tokens, cotangent, mod, sums,
-    )
-    grad_ada = jnp.einsum(
-        "vi,vko->kio", cond_part.astype(F32), grad_mod[:, :3], precision=lax.Precision.HIGHEST
-    )
+    condf = cond_part.astype(F32)
+    grad_ada = condf[0][None, :, None] * grad_mod[0, :3][:, None, :]
+    for v in range(1, cols):
+        grad_ada = grad_ada + condf[v][None, :, None] * grad_mod[v, :3][:, None, :]
     return (grad_tokens, grad_ada, grad_up, grad_down)
 
 

time: 399 us -> 339 us (0.85)
  matrix products: 67.3 us -> 46.1 us
  Pallas kernels: 287 us -> 266 us
  between operations: 14.2 us -> 0.92 us
  local copies, waits for them, and re-layouts: 15.6 us -> 3.86 us
  waiting for transfers between devices: 0.04 us -> 5.14 us
  starting transfers between devices: 0.26 us -> 4.33 us
    pallas_call x1, Pallas kernels: 31.6 us -> 7.26 us  [leave(): pl.pallas_call(functools.partial(leave_kernel, rows, cols, dps, full_widt...]
    dot_general x5 -> x4, matrix products: 45.5 us -> 27.6 us  [the longest x2 14.9 us: up_part(): lax.dot_general(mod_full, mine, (((0,), (0,)), ((), ())), preferred_eleme...]
    unnamed x10 -> x19, local copies, waits for them, and re-layouts: 15.3 us -> 0.75 us
    convert_element_type x2 -> x1, other arithmetic: 13.3 us -> 0.05 us  [time_features(): return jax.nn.silu(embed).astype(jnp.bfloat16)]
    add x0 -> x2, other arithmetic: none -> 8.17 us  [the longest x1 6.48 us: body(): grad_ada = grad_ada + condf[v][None, :, None] * grad_mod[v, :3][:, None, :]]
    ppermute x0 -> x5, waiting for transfers between devices: none -> 5.14 us  [the longest x3 5.13 us: body(): arrived.append(lax.ppermute(blocks[step], 'col', pairs))]
    ppermute x0 -> x5, starting transfers between devices: none -> 4.33 us  [the longest x3 3.83 us: body(): arrived.append(lax.ppermute(blocks[step], 'col', pairs))]
  transfers between devices with their start and end apart: 2 -> 5, of which waited for: 0 -> 2; matrix products, arithmetic and copies ran while one was open for 14% -> 6% of each run, Pallas kernels for 8% -> 0%
where the time goes in v2:
time: 339 us
  Pallas kernels  266 us (78%)
  matrix products  46.1 us (14%)
  other arithmetic  12.9 us (4%)
  waiting for transfers between devices  5.14 us (2%)
  starting transfers between devices  4.33 us (1%)
  local copies, waits for them, and re-layouts  3.86 us (1%)
    pallas_call x1, Pallas kernels, middle(): pl.pallas_call(functools.partial(middle_kernel, rows, chunks), out_shape=...  225 us
    pallas_call x1, Pallas kernels, enter(): pl.pallas_call(functools.partial(enter_kernel, rows, cols, full_width), o...  32.9 us
    dot_general x2, matrix products, up_part(): lax.dot_general(mod_full, mine, (((0,), (0,)), ((), ())), preferred_eleme...  14.9 us
    dot_general x2, matrix products, down_part(): lax.dot_general(mine, grad_full, (((0,), (0,)), ((), ())), preferred_elem...  12.7 us
    dot_general x1, matrix products, body(): branch = jnp.dot(act, down_weight, preferred_element_type=F32).astype(BF16)  9.28 us
    pallas_call x1, Pallas kernels, leave(): pl.pallas_call(functools.partial(leave_kernel, rows, cols, dps, full_widt...  7.26 us
  transfers between devices with their start and end apart: 5, of which 2 were waited for; matrix products, arithmetic and copies ran while one was open for 6% of the time, Pallas kernels for 0%

profile of v2, /device:TPU:0, one launch (start us, length us, event | category | flops | bytes accessed | tf_op | source)
XLA Modules:
  0.0 338.9 jit_solution(6267838593183319734)
XLA Ops:
  0.6 0.0 copy-start
  0.6 0.0 copy-start.1
  0.7 0.7 convert_element_type.44
  1.4 1.1 fusion.10
  2.5 0.3 multiply_cosine_fusion
  2.9 0.1 fusion.12
  2.9 3.7 %fusion.13 = f32[4,3,1024]{2,0,1:T(4,128)S(1)} fusion(bf16[3,1024,1024]{2,1,0:T(8,128)(2,1)} %param.8, bf16[4,1024]{1,0:T(4,128)(2,1)S(1)} %fusion.12), kind=kOutput, calls=%fused_computation.40 | convolution fusion | flops 25165824 | bytes 6348800 | tf_op jit(solution)/shard_map/vi,kio->vko/dot_general | solution.py:466
  6.7 0.0 copy-done
  6.7 0.0 copy-done.1
  6.7 32.9 %enter.1 = (bf16[2,4,128,1024]{3,2,1,0:T(8,128)(2,1)S(1)}, f32[8,1024]{1,0:T(8,128)S(1)}, f32[8,128]{1,0:T(8,128)S(1)}) custom-call(bf16[128,1024]{1,0:T(8,128)(2,1)S(1)} %copy-done, bf16[128,1024]{1,0:T(8,128)(2,1)S(1)} %copy-done.1, f32[4,8,1024]{2,1,0:T(8,128)S(1)} %pad.4.terms, f32[8,128]{1,0:T(8,128)S(1)} %stack.53.sums), custom_call_target="tpu_custom_call" | custom-call | tf_op jit(solution)/shard_map/enter/pallas_call | solution.py:97
  39.7 1.5 fusion.19
  41.2 0.0 slice-start
  41.2 225.5 %middle.1 = (bf16[512,4096]{1,0:T(8,128)(2,1)}, bf16[512,4096]{1,0:T(8,128)(2,1)}) custom-call(bf16[512,1024]{1,0:T(8,128)(2,1)} %bitcast.49, bf16[512,1024]{1,0:T(8,128)(2,1)} %bitcast.46, bf16[1024,4096]{1,0:T(8,128)(2,1)} %up.1, bf16[4096,1024]{1,0:T(8,128)(2,1)} %down.1), custom_call_target="tpu_custom_call" | custom-call | tf_op jit(solution)/shard_map/middle/pallas_call | solution.py:357
  266.6 0.0 slice-start.1
  266.6 0.0 copy-start.6
  266.6 9.3 %convolution_convert_fusion.3 = bf16[512,1024]{1,0:T(8,128)(2,1)S(1)} fusion(bf16[512,4096]{1,0:T(8,128)(2,1)} %get-tuple-element.30, bf16[4096,1024]{1,0:T(8,128)(2,1)} %down.1), kind=kOutput, calls=%fused_computation.12 | convolution fusion | flops 4295491584 | bytes 13631488 | tf_op jit(solution)/shard_map/dot_general | solution.py:476
  275.9 0.0 slice-done
  275.9 0.0 slice-done.1
  276.0 0.0 copy-done.6
  276.0 5.5 %convolution_convert_fusion.2 = bf16[512,1024]{1,0:T(8,128)(2,1)} fusion(bf16[512,4096]{1,0:T(8,128)(2,1)S(1)} %copy-done.6, bf16[1024,4096]{1,0:T(8,128)(2,1)S(1)} %bitcast.45), kind=kOutput, calls=%fused_computation.11 | convolution fusion | flops 4295491584 | bytes 13631488 | tf_op jit(solution)/shard_map/dot_general | solution.py:477
  281.5 0.0 copy-start.3
  281.5 1.5 dynamic-slice_bitcast_fusion
  283.0 0.8 pad_maximum_fusion.3
  283.9 0.8 pad_maximum_fusion.2
  284.7 0.8 pad_maximum_fusion.1
  285.5 0.1 pad_maximum_fusion
  285.6 0.0 copy-done.3
  285.6 0.0 copy-start.2
  285.6 0.0 copy-start.4
  285.6 6.1 %convolution_convert_fusion = bf16[1024,2048]{1,0:T(8,128)(2,1)} fusion(bf16[512,1024]{1,0:T(8,128)(2,1)S(1)} %bitcast.50, bf16[512,4096]{1,0:T(8,128)(2,1)} %get-tuple-element.31, s32[]{:T(128)S(6)} %select_n.63), kind=kOutput, calls=%fused_computation.3 | convolution fusion | flops 2149580800 | bytes 7340036 | tf_op jit(solution)/shard_map/dot_general | solution.py:500
  291.8 0.0 collective-permute-start.4
  291.8 0.0 copy-done.2
  291.8 0.0 copy-done.4
  291.8 4.7 %convolution_convert_fusion.1 = bf16[2048,1024]{1,0:T(8,128)(2,1)} fusion(bf16[512,1024]{1,0:T(8,128)(2,1)S(1)} %bitcast.47, bf16[512,4096]{1,0:T(8,128)(2,1)S(1)} %copy-done.4, s32[]{:T(128)S(6)} %select_n.63), kind=kOutput, calls=%fused_computation.4 | convolution fusion | flops 2149580800 | bytes 7340036 | tf_op jit(solution)/shard_map/dot_general | solution.py:496
  296.5 0.5 collective-permute-start.3
  297.0 0.0 collective-permute-start
  297.0 0.9 collective-permute-start.1
  297.9 2.9 collective-permute-start.2
  300.8 0.0 copy-start.5
  300.8 0.0 collective-permute-done.4
  300.8 8.8 %convert_add_fusion = f32[1024,2048]{1,0:T(8,128)} fusion(bf16[1024,2048]{1,0:T(8,128)(2,1)} %collective-permute-done.4, bf16[512,1024]{1,0:T(8,128)(2,1)S(1)} %bitcast.51, bf16[512,4096]{1,0:T(8,128)(2,1)} %get-tuple-element.31, s32[]{:T(128)S(6)} %select_n.61), kind=kOutput, calls=%fused_computation.1 | convolution fusion | flops 2151677952 | bytes 15728644 | tf_op jit(solution)/shard_map/dot_general | solution.py:500
  309.6 0.0 collective-permute-done.3
  309.6 0.0 copy-done.5
  309.6 8.0 %convert_add_fusion.1 = f32[2048,1024]{1,0:T(8,128)} fusion(bf16[2048,1024]{1,0:T(8,128)(2,1)} %collective-permute-done.3, bf16[512,1024]{1,0:T(8,128)(2,1)S(1)} %bitcast.48, bf16[512,4096]{1,0:T(8,128)(2,1)S(1)} %copy-done.5, s32[]{:T(128)S(6)} %select_n.61), kind=kOutput, calls=%fused_computation.2 | convolution fusion | flops 2151677952 | bytes 15728644 | tf_op jit(solution)/shard_map/dot_general | solution.py:496
  317.6 0.0 collective-permute-done
  317.6 4.7 %collective-permute-done.1 = bf16[2,128,1024]{2,1,0:T(8,128)(2,1)} collective-permute-done((bf16[2,128,1024]{2,1,0:T(8,128)(2,1)}, bf16[2,128,1024]{2,1,0:T(8,128)(2,1)}, u32[]{:S(2)}, u32[]{:S(2)}) %collective-permute-start.1) | collective-permute-done | bytes 524320 | tf_op jit(solution)/shard_map/ppermute | solution.py:490
  322.4 0.4 collective-permute-done.2
  322.7 1.7 convert_add_fusion.2.summed
  324.4 7.3 %leave.1 = (bf16[128,1024]{1,0:T(8,128)(2,1)S(1)}, f32[4,8,1024]{2,1,0:T(8,128)S(1)}) custom-call(f32[2,128,1024]{2,1,0:T(8,128)S(1)} %convert_add_fusion.2.summed, bf16[128,1024]{1,0:T(8,128)(2,1)S(1)} %copy-done, bf16[128,1024]{1,0:T(8,128)(2,1)S(1)} %copy-done.1, f32[8,1024]{1,0:T(8,128)S(1)} %get-tuple-element.36.mod, f32[8,128]{1,0:T(8,128)S(1)} %get-tuple-element.37.sums), custom_call_target="tpu_custom_call" | custom-call | tf_op jit(solution)/shard_map/leave/pallas_call | solution.py:434
  331.7 6.5 %multiply_add_fusion = f32[3,1024,1024]{2,1,0:T(8,128)} fusion(f32[3,1024]{1,0:T(4,128)S(1)} %get-tuple-element.55, f32[1024]{0:T(1024)S(1)} %bitcast.55, f32[3,1024]{1,0:T(4,128)S(1)} %get-tuple-element.56, f32[1024]{0:T(1024)S(1)} %bitcast.54, f32[3,1024]{1,0:T(4,128)S(1)} %get-tuple-element.57, f32[1024]{0:T(1024)S(1)} %bitcast.53, ...), kind=kLoop, calls=%fused_computation | loop fusion | flops 22020096 | bytes 12648448 | tf_op jit(solution)/shard_map/add | solution.py:522
  338.2 0.7 copy.12
  (7 shorter events, 0.1 us)
Async XLA Ops:
  0.6 6.1 %copy-start = (bf16[128,1024]{1,0:T(8,128)(2,1)S(1)}, bf16[128,1024]{1,0:T(8,128)(2,1)}, u32[]{:S(2)}) copy-start(bf16[128,1024]{1,0:T(8,128)(2,1)} %tok.3) | copy-start | bytes 786436
  0.6 6.1 %copy-start.1 = (bf16[128,1024]{1,0:T(8,128)(2,1)S(1)}, bf16[128,1024]{1,0:T(8,128)(2,1)}, u32[]{:S(2)}) copy-start(bf16[128,1024]{1,0:T(8,128)(2,1)} %cot.3) | copy-start | bytes 786436
  41.2 234.8 %slice-start = ((s8[8388608]{0:T(1024)(128)(4,1)}), s8[4194304]{0:T(1024)(128)(4,1)S(1)}, s32[]{:S(2)}) async-start(s8[8388608]{0:T(1024)(128)(4,1)} %bitcast.44), calls=%async_computation | async-start | bytes 8388608
  266.6 9.3 %slice-start.1 = ((s8[8388608]{0:T(1024)(128)(4,1)}), s8[4194304]{0:T(1024)(128)(4,1)S(1)}, s32[]{:S(2)}) async-start(s8[8388608]{0:T(1024)(128)(4,1)} %bitcast.44), calls=%async_computation.1 | async-start | bytes 8388608
  266.6 9.3 %copy-start.6 = (bf16[512,4096]{1,0:T(8,128)(2,1)S(1)}, bf16[512,4096]{1,0:T(8,128)(2,1)}, u32[]{:S(2)}) copy-start(bf16[512,4096]{1,0:T(8,128)(2,1)} %get-tuple-element.31) | copy-start | bytes 12582916
  281.5 4.1 %copy-start.3 = (bf16[1,4,128,1024]{3,2,1,0:T(8,128)(2,1)S(1)}, bf16[1,4,128,1024]{3,2,1,0:T(8,128)(2,1)}, u32[]{:S(2)}) copy-start(bf16[1,4,128,1024]{3,2,1,0:T(8,128)(2,1)} %get-tuple-element.45) | copy-start | bytes 3145732
  285.6 6.2 %copy-start.2 = (bf16[1,4,128,1024]{3,2,1,0:T(8,128)(2,1)S(1)}, bf16[1,4,128,1024]{3,2,1,0:T(8,128)(2,1)}, u32[]{:S(2)}) copy-start(bf16[1,4,128,1024]{3,2,1,0:T(8,128)(2,1)} %get-tuple-element.44) | copy-start | bytes 3145732
  285.6 6.2 %copy-start.4 = (bf16[512,4096]{1,0:T(8,128)(2,1)S(1)}, bf16[512,4096]{1,0:T(8,128)(2,1)}, u32[]{:S(2)}) copy-start(bf16[512,4096]{1,0:T(8,128)(2,1)} %get-tuple-element.30) | copy-start | bytes 12582916
  291.8 9.0 %collective-permute-start.4 = (bf16[1024,2048]{1,0:T(8,128)(2,1)}, bf16[1024,2048]{1,0:T(8,128)(2,1)}, u32[]{:S(2)}, u32[]{:S(2)}) collective-permute-start(bf16[1024,2048]{1,0:T(8,128)(2,1)} %convolution_convert_fusion), channel_id=1, source_target_pairs={{0,1},{1,0},{2,3},{3,2},{4,5},{5,4},{6,7},{7,6},{8,9},{9,8},{10,11... | collective-permute-start | bytes 12582920 | tf_op jit(solution)/shard_map/ppermute | solution.py:507
  296.5 13.1 %collective-permute-start.3 = (bf16[2048,1024]{1,0:T(8,128)(2,1)}, bf16[2048,1024]{1,0:T(8,128)(2,1)}, u32[]{:S(2)}, u32[]{:S(2)}) collective-permute-start(bf16[2048,1024]{1,0:T(8,128)(2,1)} %convolution_convert_fusion.1), channel_id=1, source_target_pairs={{0,1},{1,0},{2,3},{3,2},{4,5},{5,4},{6,7},{7,6},{8,9},{9,8},{10,11... | collective-permute-start | bytes 12582920 | tf_op jit(solution)/shard_map/ppermute | solution.py:507
  297.0 20.7 %collective-permute-start = (bf16[2,128,1024]{2,1,0:T(8,128)(2,1)}, bf16[2,128,1024]{2,1,0:T(8,128)(2,1)}, u32[]{:S(2)}, u32[]{:S(2)}) collective-permute-start(bf16[2,128,1024]{2,1,0:T(8,128)(2,1)} %pad_maximum_fusion.1), channel_id=1, source_target_pairs={{0,2},{2,4},{4,6},{6,0},{1,3},{3,5},{5,7},{7,1},{8,10},{10,12},{12... | collective-permute-start | bytes 1572872 | tf_op jit(solution)/shard_map/ppermute | solution.py:490
  297.0 25.4 %collective-permute-start.1 = (bf16[2,128,1024]{2,1,0:T(8,128)(2,1)}, bf16[2,128,1024]{2,1,0:T(8,128)(2,1)}, u32[]{:S(2)}, u32[]{:S(2)}) collective-permute-start(bf16[2,128,1024]{2,1,0:T(8,128)(2,1)} %pad_maximum_fusion.2), channel_id=1, source_target_pairs={{0,4},{2,6},{4,0},{6,2},{1,5},{3,7},{5,1},{7,3},{8,12},{10,14},{12... | collective-permute-start | bytes 1572872 | tf_op jit(solution)/shard_map/ppermute | solution.py:490
  297.9 24.9 %collective-permute-start.2 = (bf16[2,128,1024]{2,1,0:T(8,128)(2,1)}, bf16[2,128,1024]{2,1,0:T(8,128)(2,1)}, u32[]{:S(2)}, u32[]{:S(2)}) collective-permute-start(bf16[2,128,1024]{2,1,0:T(8,128)(2,1)} %pad_maximum_fusion.3), channel_id=1, source_target_pairs={{0,6},{2,0},{4,2},{6,4},{1,7},{3,1},{5,3},{7,5},{8,14},{10,8},{12,... | collective-permute-start | bytes 1572872 | tf_op jit(solution)/shard_map/ppermute | solution.py:490
  300.8 8.8 %copy-start.5 = (bf16[512,4096]{1,0:T(8,128)(2,1)S(1)}, bf16[512,4096]{1,0:T(8,128)(2,1)}, u32[]{:S(2)}) copy-start(bf16[512,4096]{1,0:T(8,128)(2,1)} %get-tuple-element.30) | copy-start | bytes 12582916
